TPU v7x, 32 devices: a whole 2x2x4 slice. The times are simulated.
32 devices in a mesh: rot: 8 (over z, y), fft: 4 (over x, core).
Axes of the slice: x: 2, y: 2, z: 4, core: 2. Of those that a mesh axis runs over, the one named last changes fastest.
Arguments:
- receptor: bfloat16 [2, 11, 128, 128, 128], P(None, None, 'fft'), may hold values from -6 to 6, as said below
- ligand_grids: bfloat16 [32, 11, 32, 1024], P(None, None, 'fft'), may hold values from -8 to 8
- rot_index: int32 [48], P('rot'), parts along dimension 0, may hold values from 0 to 31
Outputs:
- scores: float32 [48, 128, 128, 128], P('rot', 'fft'), parts along dimension 0
- best: float32 [48], P('rot'), parts along dimension 0
There are 8 independent parts, one for each index of `rot`. A program takes and returns all parts, laid end to end along the dimension named above; an argument that names none is the same for every part. Nothing has to cross between parts.
Inputs may be any that keep to these rules, and one draw needn't show every extreme that they name: The receptor spectra are those of real grids: in every channel the entry at frequency (-kz, -kx, -ky), taken modulo 128 along each dimension, is the complex conjugate of the entry at (kz, kx, ky).
All inputs are finite; a program needn't handle non-finite values.
Results may differ from a plain program's by a relative error of at most 0.0003.
Values may be sent and summed in bfloat16 or wider, within the bound.
A program may use at most 256 MiB of HBM per device.

v0:
```python
import math
import jax
import jax.numpy as jnp
from jax import lax
from jax.sharding import PartitionSpec as P

TRIPLE = lax.Precision.HIGH


def phase_table(row_index, col_index, length):
    turns = row_index[:, None] * col_index[None, :] % length
    angle = turns.astype(jnp.float32) * (2.0 * math.pi / length)
    return (jnp.cos(angle), jnp.sin(angle))


def split_table(table):
    upper = table.astype(jnp.bfloat16)
    widened = lax.optimization_barrier(upper).astype(jnp.float32)
    return (upper, (table - widened).astype(jnp.bfloat16))


def contract(form, left, right):
    return jnp.einsum(form, left, right, precision=TRIPLE)


def narrow_contract(form, values, table_pair):
    upper = jnp.einsum(form, values, table_pair[0], preferred_element_type=jnp.float32)
    lower = jnp.einsum(form, values, table_pair[1], preferred_element_type=jnp.float32)
    return upper + lower


def shards(receptor, ligand_grids, rot_index):
    groups = lax.axis_size("fft")
    slab_depth = receptor.shape[2]
    length = receptor.shape[3]
    channels = receptor.shape[1]
    box_cells = ligand_grids.shape[2] * groups
    rotations = rot_index.shape[0]
    freq_slab = lax.axis_index("fft") * slab_depth + jnp.arange(slab_depth, dtype=jnp.int32)
    freq_all = jnp.arange(length, dtype=jnp.int32)
    cos_box, sin_box = phase_table(jnp.arange(box_cells, dtype=jnp.int32), freq_all, length)
    cos_full, sin_full = phase_table(freq_all, freq_all, length)
    inverse_volume = 1.0 / float(length) ** 3
    chosen = jnp.take(ligand_grids, rot_index, axis=0)
    empty = jnp.zeros((rotations, channels, slab_depth, ligand_grids.shape[3]), jnp.float32)
    planes = lax.all_gather(chosen, "fft", axis=2, tiled=True)
    plane_index = jnp.arange(planes.shape[2], dtype=jnp.int32)
    cos_depth, sin_depth = phase_table(plane_index, freq_slab, length)
    slab_real = narrow_contract("rczp,zk->rckp", planes, split_table(cos_depth))
    slab_imag = (empty, empty)[1] - narrow_contract("rczp,zk->rckp", planes, split_table(sin_depth))

    def ligand_product(one_real, one_imag):
        grid_real = one_real.reshape(channels, slab_depth, box_cells, box_cells)
        grid_imag = one_imag.reshape(channels, slab_depth, box_cells, box_cells)
        half_real = contract("ckxy,yb->ckxb", grid_real, cos_box) + contract(
            "ckxy,yb->ckxb", grid_imag, sin_box
        )
        half_imag = contract("ckxy,yb->ckxb", grid_imag, cos_box) - contract(
            "ckxy,yb->ckxb", grid_real, sin_box
        )
        spec_real = contract("ckxb,xa->ckab", half_real, cos_box) + contract(
            "ckxb,xa->ckab", half_imag, sin_box
        )
        spec_imag = contract("ckxb,xa->ckab", half_imag, cos_box) - contract(
            "ckxb,xa->ckab", half_real, sin_box
        )
        prod_real = jnp.sum(receptor[0] * spec_real + receptor[1] * spec_imag, axis=0)
        prod_imag = jnp.sum(receptor[1] * spec_real - receptor[0] * spec_imag, axis=0)
        return (prod_real, prod_imag)

    def inverse_plane(prod_real, prod_imag):
        rows_real = contract("kay,yb->kab", prod_real, cos_full) - contract(
            "kay,yb->kab", prod_imag, sin_full
        )
        rows_imag = contract("kay,yb->kab", prod_imag, cos_full) + contract(
            "kay,yb->kab", prod_real, sin_full
        )
        grid_real = contract("kab,ax->kxb", rows_real, cos_full) - contract(
            "kab,ax->kxb", rows_imag, sin_full
        )
        grid_imag = contract("kab,ax->kxb", rows_imag, cos_full) + contract(
            "kab,ax->kxb", rows_real, sin_full
        )
        return (grid_real, grid_imag)

    def one_rotation(single):
        prod_real, prod_imag = ligand_product(single[0], single[1])
        return inverse_plane(prod_real, prod_imag)

    planes_real, planes_imag = lax.map(one_rotation, (slab_real, slab_imag))
    part_real = lax.all_to_all(planes_real, "fft", split_axis=2, concat_axis=1, tiled=True)
    part_imag = lax.all_to_all(planes_imag, "fft", split_axis=2, concat_axis=1, tiled=True)
    field = contract("rkxy,kz->rxyz", part_real, cos_full) - contract(
        "rkxy,kz->rxyz", part_imag, sin_full
    )
    scores = field * inverse_volume
    best = lax.pmin(jnp.min(scores, axis=(1, 2, 3)), "fft")
    return (scores, best)


def solution(mesh):
    placed = (P(None, None, "fft", None, None), P(None, None, "fft", None), P("rot"))
    return jax.shard_map(
        shards,
        mesh=mesh,
        in_specs=placed,
        out_specs=(P("rot", "fft", None, None), P("rot")),
        check_vma=False,
    )
```

profile of v0, /device:TPU:0, one launch (start us, length us, event | category | flops | bytes accessed | tf_op | source)
XLA Modules:
  0.0 1411.9 jit_solution(3870738557738267873)
XLA Ops:
  13.2 29.4 %copy.31 = bf16[2,11,32,128,128]{3,4,2,1,0:T(8,128)(2,1)} copy(bf16[2,11,32,128,128]{4,3,2,1,0:T(8,128)(2,1)} %param.5) | data formatting | bytes 46137344
  42.5 8.5 all-gather.2.cloned.1.call-done
  51.1 3.8 fusion.164
  56.3 4.7 add_bitcast_fusion.1
  61.0 4.7 subtract_bitcast_fusion.1
  65.7 996.6 %while.14 = (s32[]{:T(128)}, f32[6,32,128,128]{3,1,0,2:T(8,128)}, f32[6,32,128,128]{3,1,0,2:T(8,128)}, bf16[2,11,32,128,128]{3,4,2,1,0:T(8,128)(2,1)}, f32[6,11,...) while((s32[]{:T(128)}, f32[6,32,128,128]{3,1,0,2:T(8,128)}, ...), condition=%wide.region_3.4_spmd.clone.clone, body=%wide.region_0.3_spmd.clone.clone.sunk | while | flops 8833138688 | bytes 390595392 | solution.py:90
  71.0 7.6 fusion.291
  83.7 7.0 convolution_add_fusion.4
  90.7 21.8 %fusion.292 = f32[11,32,128,128]{3,2,1,0:T(8,128)} fusion(f32[11,32,32,128]{3,2,1,0:T(8,128)S(1)} %convolution_add_fusion.4), kind=kOutput, calls=%fused_computation.48.clone.1 | convolution fusion | flops 1107353600 | bytes 28835840 | tf_op jit(solution)/shard_map/while/body/eval_jaxpr/ckxb,xa->ckab/dot_general | solution.py:23
  112.4 21.3 %fusion.293 = f32[11,32,128,128]{3,2,1,0:T(8,128)} fusion(f32[11,32,32,128]{3,2,1,0:T(8,128)S(1)} %convolution_add_fusion.4), kind=kOutput, calls=%fused_computation.58.clone.1 | convolution fusion | flops 1107353600 | bytes 28835840 | tf_op jit(solution)/shard_map/while/body/eval_jaxpr/ckxb,xa->ckab/dot_general | solution.py:23
  138.8 21.2 %fusion.295 = f32[11,32,128,128]{3,2,1,0:T(8,128)} fusion(f32[11,32,32,128]{3,2,1,0:T(8,128)S(1)} %convolution_subtract_fusion.4), kind=kOutput, calls=%fused_computation.50.clone.1 | convolution fusion | flops 1107353600 | bytes 28835840 | tf_op jit(solution)/shard_map/while/body/eval_jaxpr/ckxb,xa->ckab/dot_general | solution.py:23
  160.0 37.3 %fusion.296 = (f32[32,128,128]{1,2,0:T(8,128)}, f32[32,128,128]{1,2,0:T(8,128)S(1)}) fusion(f32[11,32,128,128]{3,2,1,0:T(8,128)} %fusion.292, bf16[2,11,32,128,128]{3,4,2,1,0:T(8,128)(2,1)} %get-tuple-element.251, f32[11,32,128,128]{3,2,1,0:T(8,128)} %fusion.293, f32[11,32,128,128]{3,2,1,0:T(8,128)} %fusion.295, f32[11,32,32,128]{3,2,1,0:T(8,128)} %copy-done), kind=kOutput, calls=%fused_computation.12.clone.1 | convolution fusion | flops 1175511040 | bytes 102236160 | tf_op jit(solution)/shard_map/while/body/eval_jaxpr/ckxb,xa->ckab/dot_general | solution.py:23
  199.3 3.7 convolution_subtract_fusion.5
  210.3 3.7 subtract_bitcast_fusion.3
  226.6 4.0 constant_dynamic-update-slice_fusion.3
  235.7 7.6 fusion.291
  248.4 7.0 convolution_add_fusion.4
  255.4 21.4 %fusion.292 = f32[11,32,128,128]{3,2,1,0:T(8,128)} fusion(f32[11,32,32,128]{3,2,1,0:T(8,128)S(1)} %convolution_add_fusion.4), kind=kOutput, calls=%fused_computation.48.clone.1 | convolution fusion | flops 1107353600 | bytes 28835840 | tf_op jit(solution)/shard_map/while/body/eval_jaxpr/ckxb,xa->ckab/dot_general | solution.py:23
  276.9 21.6 %fusion.293 = f32[11,32,128,128]{3,2,1,0:T(8,128)} fusion(f32[11,32,32,128]{3,2,1,0:T(8,128)S(1)} %convolution_add_fusion.4), kind=kOutput, calls=%fused_computation.58.clone.1 | convolution fusion | flops 1107353600 | bytes 28835840 | tf_op jit(solution)/shard_map/while/body/eval_jaxpr/ckxb,xa->ckab/dot_general | solution.py:23
  303.6 21.2 %fusion.295 = f32[11,32,128,128]{3,2,1,0:T(8,128)} fusion(f32[11,32,32,128]{3,2,1,0:T(8,128)S(1)} %convolution_subtract_fusion.4), kind=kOutput, calls=%fused_computation.50.clone.1 | convolution fusion | flops 1107353600 | bytes 28835840 | tf_op jit(solution)/shard_map/while/body/eval_jaxpr/ckxb,xa->ckab/dot_general | solution.py:23
  324.8 37.2 %fusion.296 = (f32[32,128,128]{1,2,0:T(8,128)}, f32[32,128,128]{1,2,0:T(8,128)S(1)}) fusion(f32[11,32,128,128]{3,2,1,0:T(8,128)} %fusion.292, bf16[2,11,32,128,128]{3,4,2,1,0:T(8,128)(2,1)} %get-tuple-element.251, f32[11,32,128,128]{3,2,1,0:T(8,128)} %fusion.293, f32[11,32,128,128]{3,2,1,0:T(8,128)} %fusion.295, f32[11,32,32,128]{3,2,1,0:T(8,128)} %copy-done), kind=kOutput, calls=%fused_computation.12.clone.1 | convolution fusion | flops 1175511040 | bytes 102236160 | tf_op jit(solution)/shard_map/while/body/eval_jaxpr/ckxb,xa->ckab/dot_general | solution.py:23
  364.0 3.7 convolution_subtract_fusion.5
  391.1 4.0 constant_dynamic-update-slice_fusion.3
  400.3 7.6 fusion.291
  413.0 7.0 convolution_add_fusion.4
  420.0 21.7 %fusion.292 = f32[11,32,128,128]{3,2,1,0:T(8,128)} fusion(f32[11,32,32,128]{3,2,1,0:T(8,128)S(1)} %convolution_add_fusion.4), kind=kOutput, calls=%fused_computation.48.clone.1 | convolution fusion | flops 1107353600 | bytes 28835840 | tf_op jit(solution)/shard_map/while/body/eval_jaxpr/ckxb,xa->ckab/dot_general | solution.py:23
  441.7 21.3 %fusion.293 = f32[11,32,128,128]{3,2,1,0:T(8,128)} fusion(f32[11,32,32,128]{3,2,1,0:T(8,128)S(1)} %convolution_add_fusion.4), kind=kOutput, calls=%fused_computation.58.clone.1 | convolution fusion | flops 1107353600 | bytes 28835840 | tf_op jit(solution)/shard_map/while/body/eval_jaxpr/ckxb,xa->ckab/dot_general | solution.py:23
  468.1 21.2 %fusion.295 = f32[11,32,128,128]{3,2,1,0:T(8,128)} fusion(f32[11,32,32,128]{3,2,1,0:T(8,128)S(1)} %convolution_subtract_fusion.4), kind=kOutput, calls=%fused_computation.50.clone.1 | convolution fusion | flops 1107353600 | bytes 28835840 | tf_op jit(solution)/shard_map/while/body/eval_jaxpr/ckxb,xa->ckab/dot_general | solution.py:23
  489.3 37.3 %fusion.296 = (f32[32,128,128]{1,2,0:T(8,128)}, f32[32,128,128]{1,2,0:T(8,128)S(1)}) fusion(f32[11,32,128,128]{3,2,1,0:T(8,128)} %fusion.292, bf16[2,11,32,128,128]{3,4,2,1,0:T(8,128)(2,1)} %get-tuple-element.251, f32[11,32,128,128]{3,2,1,0:T(8,128)} %fusion.293, f32[11,32,128,128]{3,2,1,0:T(8,128)} %fusion.295, f32[11,32,32,128]{3,2,1,0:T(8,128)} %copy-done), kind=kOutput, calls=%fused_computation.12.clone.1 | convolution fusion | flops 1175511040 | bytes 102236160 | tf_op jit(solution)/shard_map/while/body/eval_jaxpr/ckxb,xa->ckab/dot_general | solution.py:23
  528.6 3.7 convolution_subtract_fusion.5
  539.6 3.7 subtract_bitcast_fusion.3
  555.9 4.0 constant_dynamic-update-slice_fusion.3
  565.0 7.6 fusion.291
  577.7 7.0 convolution_add_fusion.4
  584.7 21.4 %fusion.292 = f32[11,32,128,128]{3,2,1,0:T(8,128)} fusion(f32[11,32,32,128]{3,2,1,0:T(8,128)S(1)} %convolution_add_fusion.4), kind=kOutput, calls=%fused_computation.48.clone.1 | convolution fusion | flops 1107353600 | bytes 28835840 | tf_op jit(solution)/shard_map/while/body/eval_jaxpr/ckxb,xa->ckab/dot_general | solution.py:23
  606.2 21.6 %fusion.293 = f32[11,32,128,128]{3,2,1,0:T(8,128)} fusion(f32[11,32,32,128]{3,2,1,0:T(8,128)S(1)} %convolution_add_fusion.4), kind=kOutput, calls=%fused_computation.58.clone.1 | convolution fusion | flops 1107353600 | bytes 28835840 | tf_op jit(solution)/shard_map/while/body/eval_jaxpr/ckxb,xa->ckab/dot_general | solution.py:23
  632.8 21.2 %fusion.295 = f32[11,32,128,128]{3,2,1,0:T(8,128)} fusion(f32[11,32,32,128]{3,2,1,0:T(8,128)S(1)} %convolution_subtract_fusion.4), kind=kOutput, calls=%fused_computation.50.clone.1 | convolution fusion | flops 1107353600 | bytes 28835840 | tf_op jit(solution)/shard_map/while/body/eval_jaxpr/ckxb,xa->ckab/dot_general | solution.py:23
  654.1 37.2 %fusion.296 = (f32[32,128,128]{1,2,0:T(8,128)}, f32[32,128,128]{1,2,0:T(8,128)S(1)}) fusion(f32[11,32,128,128]{3,2,1,0:T(8,128)} %fusion.292, bf16[2,11,32,128,128]{3,4,2,1,0:T(8,128)(2,1)} %get-tuple-element.251, f32[11,32,128,128]{3,2,1,0:T(8,128)} %fusion.293, f32[11,32,128,128]{3,2,1,0:T(8,128)} %fusion.295, f32[11,32,32,128]{3,2,1,0:T(8,128)} %copy-done), kind=kOutput, calls=%fused_computation.12.clone.1 | convolution fusion | flops 1175511040 | bytes 102236160 | tf_op jit(solution)/shard_map/while/body/eval_jaxpr/ckxb,xa->ckab/dot_general | solution.py:23
  693.3 3.7 convolution_subtract_fusion.5
  720.4 4.0 constant_dynamic-update-slice_fusion.3
  729.6 7.6 fusion.291
  742.3 7.0 convolution_add_fusion.4
  749.3 21.7 %fusion.292 = f32[11,32,128,128]{3,2,1,0:T(8,128)} fusion(f32[11,32,32,128]{3,2,1,0:T(8,128)S(1)} %convolution_add_fusion.4), kind=kOutput, calls=%fused_computation.48.clone.1 | convolution fusion | flops 1107353600 | bytes 28835840 | tf_op jit(solution)/shard_map/while/body/eval_jaxpr/ckxb,xa->ckab/dot_general | solution.py:23
  771.0 21.3 %fusion.293 = f32[11,32,128,128]{3,2,1,0:T(8,128)} fusion(f32[11,32,32,128]{3,2,1,0:T(8,128)S(1)} %convolution_add_fusion.4), kind=kOutput, calls=%fused_computation.58.clone.1 | convolution fusion | flops 1107353600 | bytes 28835840 | tf_op jit(solution)/shard_map/while/body/eval_jaxpr/ckxb,xa->ckab/dot_general | solution.py:23
  797.4 21.2 %fusion.295 = f32[11,32,128,128]{3,2,1,0:T(8,128)} fusion(f32[11,32,32,128]{3,2,1,0:T(8,128)S(1)} %convolution_subtract_fusion.4), kind=kOutput, calls=%fused_computation.50.clone.1 | convolution fusion | flops 1107353600 | bytes 28835840 | tf_op jit(solution)/shard_map/while/body/eval_jaxpr/ckxb,xa->ckab/dot_general | solution.py:23
  818.6 37.3 %fusion.296 = (f32[32,128,128]{1,2,0:T(8,128)}, f32[32,128,128]{1,2,0:T(8,128)S(1)}) fusion(f32[11,32,128,128]{3,2,1,0:T(8,128)} %fusion.292, bf16[2,11,32,128,128]{3,4,2,1,0:T(8,128)(2,1)} %get-tuple-element.251, f32[11,32,128,128]{3,2,1,0:T(8,128)} %fusion.293, f32[11,32,128,128]{3,2,1,0:T(8,128)} %fusion.295, f32[11,32,32,128]{3,2,1,0:T(8,128)} %copy-done), kind=kOutput, calls=%fused_computation.12.clone.1 | convolution fusion | flops 1175511040 | bytes 102236160 | tf_op jit(solution)/shard_map/while/body/eval_jaxpr/ckxb,xa->ckab/dot_general | solution.py:23
  857.9 3.7 convolution_subtract_fusion.5
  868.8 3.7 subtract_bitcast_fusion.3
  885.1 4.0 constant_dynamic-update-slice_fusion.3
  894.3 7.6 fusion.291
  907.0 7.0 convolution_add_fusion.4
  914.0 21.4 %fusion.292 = f32[11,32,128,128]{3,2,1,0:T(8,128)} fusion(f32[11,32,32,128]{3,2,1,0:T(8,128)S(1)} %convolution_add_fusion.4), kind=kOutput, calls=%fused_computation.48.clone.1 | convolution fusion | flops 1107353600 | bytes 28835840 | tf_op jit(solution)/shard_map/while/body/eval_jaxpr/ckxb,xa->ckab/dot_general | solution.py:23
  935.4 21.6 %fusion.293 = f32[11,32,128,128]{3,2,1,0:T(8,128)} fusion(f32[11,32,32,128]{3,2,1,0:T(8,128)S(1)} %convolution_add_fusion.4), kind=kOutput, calls=%fused_computation.58.clone.1 | convolution fusion | flops 1107353600 | bytes 28835840 | tf_op jit(solution)/shard_map/while/body/eval_jaxpr/ckxb,xa->ckab/dot_general | solution.py:23
  962.1 21.2 %fusion.295 = f32[11,32,128,128]{3,2,1,0:T(8,128)} fusion(f32[11,32,32,128]{3,2,1,0:T(8,128)S(1)} %convolution_subtract_fusion.4), kind=kOutput, calls=%fused_computation.50.clone.1 | convolution fusion | flops 1107353600 | bytes 28835840 | tf_op jit(solution)/shard_map/while/body/eval_jaxpr/ckxb,xa->ckab/dot_general | solution.py:23
  983.3 37.2 %fusion.296 = (f32[32,128,128]{1,2,0:T(8,128)}, f32[32,128,128]{1,2,0:T(8,128)S(1)}) fusion(f32[11,32,128,128]{3,2,1,0:T(8,128)} %fusion.292, bf16[2,11,32,128,128]{3,4,2,1,0:T(8,128)(2,1)} %get-tuple-element.251, f32[11,32,128,128]{3,2,1,0:T(8,128)} %fusion.293, f32[11,32,128,128]{3,2,1,0:T(8,128)} %fusion.295, f32[11,32,32,128]{3,2,1,0:T(8,128)} %copy-done), kind=kOutput, calls=%fused_computation.12.clone.1 | convolution fusion | flops 1175511040 | bytes 102236160 | tf_op jit(solution)/shard_map/while/body/eval_jaxpr/ckxb,xa->ckab/dot_general | solution.py:23
  1049.6 4.0 constant_dynamic-update-slice_fusion.3
  1062.4 147.4 %all_to_all.36 = f32[6,32,128,128]{3,1,0,2:T(8,128)} all-to-all(f32[6,32,128,128]{3,1,0,2:T(8,128)} %get-tuple-element.92), channel_id=1, replica_groups=mesh['rot'=8,'fft'=4] {'fft'}, dimensions={2} | all-to-all | bytes 25165824 | tf_op jit(solution)/shard_map/all_to_all | solution.py:92
  1209.8 6.3 all-to-all-start
  1216.1 20.0 %copy.38 = f32[6,4,32,32,128]{4,3,2,1,0:T(8,128)} copy(f32[6,4,32,32,128]{4,2,0,3,1:T(8,128)} %bitcast.214) | data formatting | bytes 25165824 | tf_op jit(solution)/shard_map/all_to_all | solution.py:92
  1236.1 22.9 %fusion.134 = f32[6,32,128,128]{3,2,1,0:T(8,128)} fusion(f32[6,128,32,128]{3,2,1,0:T(8,128)} %bitcast.213), kind=kOutput, calls=%fused_computation.135 | convolution fusion | flops 2416148480 | bytes 25165824 | tf_op jit(solution)/shard_map/rkxy,kz->rxyz/dot_general | solution.py:23
  1258.9 95.3 %all-to-all-done = f32[6,32,128,128]{3,1,0,2:T(8,128)} async-done(((f32[6,32,128,128]{3,1,0,2:T(8,128)}), f32[6,32,128,128]{3,1,0,2:T(8,128)}, u32[]{:S(2)}, u32[]{:S(2)}) %all-to-all-start) | async-done | bytes 12582944 | tf_op jit(solution)/shard_map/all_to_all | solution.py:91
  1354.2 20.0 %copy.34 = f32[6,4,32,32,128]{4,3,2,1,0:T(8,128)} copy(f32[6,4,32,32,128]{4,2,0,3,1:T(8,128)} %bitcast.12) | data formatting | bytes 25165824 | tf_op jit(solution)/shard_map/all_to_all | solution.py:91
  1374.2 24.5 %fusion.198 = (f32[6]{0:T(128)S(1)}, f32[6,32,128,128]{3,2,1,0:T(8,128)}) fusion(f32[6,32,128,128]{3,2,1,0:T(8,128)} %fusion.134, f32[6,128,32,128]{3,2,1,0:T(8,128)} %bitcast.212), kind=kOutput, calls=%fused_computation.205 | convolution fusion | flops 2425585664 | bytes 37748760 | tf_op jit(solution)/shard_map/rkxy,kz->rxyz/dot_general | solution.py:23
  1398.6 6.2 pmin.7
  (222 shorter events, 242.2 us)
Async XLA Ops:
  7.2 43.9 %all-gather.2.cloned.1.call-start = ((), (), s32[]{:S(2)}) async-start(), calls=%async_computation.2 | async-start | bytes 5406720 | tf_op jit(solution)/shard_map/all_gather | solution.py:46
  51.1 3.8 copy-start.5
  90.7 43.1 %slice-start.2 = ((s8[5767168]{0:T(1024)(128)(4,1)}), s8[4194304]{0:T(1024)(128)(4,1)S(1)}, s32[]{:S(2)}) async-start(s8[5767168]{0:T(1024)(128)(4,1)} %bitcast.210), calls=%async_computation.5 | async-start | bytes 8388608 | tf_op jit(solution)/shard_map/while
  90.7 45.6 %slice-start = ((s8[5767168]{0:T(1024)(128)(4,1)}), s8[4194304]{0:T(1024)(128)(4,1)S(1)}, s32[]{:S(2)}) async-start(s8[5767168]{0:T(1024)(128)(4,1)} %bitcast.208), calls=%async_computation.3 | async-start | bytes 8388608 | tf_op jit(solution)/shard_map/while
  112.4 21.3 %slice-start.3 = ((s8[5767168]{0:T(1024)(128)(4,1)}), s8[1572864]{0:T(1024)(128)(4,1)S(1)}, s32[]{:S(2)}) async-start(s8[5767168]{0:T(1024)(128)(4,1)} %bitcast.210), calls=%async_computation.6 | async-start | bytes 3145728 | tf_op jit(solution)/shard_map/while
  112.4 23.9 %slice-start.1 = ((s8[5767168]{0:T(1024)(128)(4,1)}), s8[1572864]{0:T(1024)(128)(4,1)S(1)}, s32[]{:S(2)}) async-start(s8[5767168]{0:T(1024)(128)(4,1)} %bitcast.208), calls=%async_computation.4 | async-start | bytes 3145728 | tf_op jit(solution)/shard_map/while
  138.8 21.2 %copy-start = (f32[11,32,32,128]{3,2,1,0:T(8,128)}, f32[11,32,32,128]{3,2,1,0:T(8,128)S(1)}, u32[]{:S(2)}) copy-start(f32[11,32,32,128]{3,2,1,0:T(8,128)S(1)} %convolution_subtract_fusion.4) | copy-start | bytes 17301508 | tf_op jit(solution)/shard_map/while
  199.3 5.7 copy-start.1
  203.0 5.9 copy-start.2
  209.0 1.3 copy-start.4
  214.0 6.8 copy-start.3
  255.4 43.1 %slice-start.2 = ((s8[5767168]{0:T(1024)(128)(4,1)}), s8[4194304]{0:T(1024)(128)(4,1)S(1)}, s32[]{:S(2)}) async-start(s8[5767168]{0:T(1024)(128)(4,1)} %bitcast.210), calls=%async_computation.5 | async-start | bytes 8388608 | tf_op jit(solution)/shard_map/while
  255.4 45.6 %slice-start = ((s8[5767168]{0:T(1024)(128)(4,1)}), s8[4194304]{0:T(1024)(128)(4,1)S(1)}, s32[]{:S(2)}) async-start(s8[5767168]{0:T(1024)(128)(4,1)} %bitcast.208), calls=%async_computation.3 | async-start | bytes 8388608 | tf_op jit(solution)/shard_map/while
  276.9 21.6 %slice-start.3 = ((s8[5767168]{0:T(1024)(128)(4,1)}), s8[1572864]{0:T(1024)(128)(4,1)S(1)}, s32[]{:S(2)}) async-start(s8[5767168]{0:T(1024)(128)(4,1)} %bitcast.210), calls=%async_computation.6 | async-start | bytes 3145728 | tf_op jit(solution)/shard_map/while
  276.9 24.2 %slice-start.1 = ((s8[5767168]{0:T(1024)(128)(4,1)}), s8[1572864]{0:T(1024)(128)(4,1)S(1)}, s32[]{:S(2)}) async-start(s8[5767168]{0:T(1024)(128)(4,1)} %bitcast.208), calls=%async_computation.4 | async-start | bytes 3145728 | tf_op jit(solution)/shard_map/while
  303.5 21.2 %copy-start = (f32[11,32,32,128]{3,2,1,0:T(8,128)}, f32[11,32,32,128]{3,2,1,0:T(8,128)S(1)}, u32[]{:S(2)}) copy-start(f32[11,32,32,128]{3,2,1,0:T(8,128)S(1)} %convolution_subtract_fusion.4) | copy-start | bytes 17301508 | tf_op jit(solution)/shard_map/while
  364.0 5.7 copy-start.1
  367.7 5.9 copy-start.2
  373.7 1.3 copy-start.4
  378.5 6.8 copy-start.3
  420.0 43.0 %slice-start.2 = ((s8[5767168]{0:T(1024)(128)(4,1)}), s8[4194304]{0:T(1024)(128)(4,1)S(1)}, s32[]{:S(2)}) async-start(s8[5767168]{0:T(1024)(128)(4,1)} %bitcast.210), calls=%async_computation.5 | async-start | bytes 8388608 | tf_op jit(solution)/shard_map/while
  420.0 45.6 %slice-start = ((s8[5767168]{0:T(1024)(128)(4,1)}), s8[4194304]{0:T(1024)(128)(4,1)S(1)}, s32[]{:S(2)}) async-start(s8[5767168]{0:T(1024)(128)(4,1)} %bitcast.208), calls=%async_computation.3 | async-start | bytes 8388608 | tf_op jit(solution)/shard_map/while
  441.7 21.3 %slice-start.3 = ((s8[5767168]{0:T(1024)(128)(4,1)}), s8[1572864]{0:T(1024)(128)(4,1)S(1)}, s32[]{:S(2)}) async-start(s8[5767168]{0:T(1024)(128)(4,1)} %bitcast.210), calls=%async_computation.6 | async-start | bytes 3145728 | tf_op jit(solution)/shard_map/while
  441.7 23.9 %slice-start.1 = ((s8[5767168]{0:T(1024)(128)(4,1)}), s8[1572864]{0:T(1024)(128)(4,1)S(1)}, s32[]{:S(2)}) async-start(s8[5767168]{0:T(1024)(128)(4,1)} %bitcast.208), calls=%async_computation.4 | async-start | bytes 3145728 | tf_op jit(solution)/shard_map/while
  468.1 21.2 %copy-start = (f32[11,32,32,128]{3,2,1,0:T(8,128)}, f32[11,32,32,128]{3,2,1,0:T(8,128)S(1)}, u32[]{:S(2)}) copy-start(f32[11,32,32,128]{3,2,1,0:T(8,128)S(1)} %convolution_subtract_fusion.4) | copy-start | bytes 17301508 | tf_op jit(solution)/shard_map/while
  528.6 5.7 copy-start.1
  532.3 5.9 copy-start.2
  538.2 1.3 copy-start.4
  543.3 6.8 copy-start.3
  584.7 43.1 %slice-start.2 = ((s8[5767168]{0:T(1024)(128)(4,1)}), s8[4194304]{0:T(1024)(128)(4,1)S(1)}, s32[]{:S(2)}) async-start(s8[5767168]{0:T(1024)(128)(4,1)} %bitcast.210), calls=%async_computation.5 | async-start | bytes 8388608 | tf_op jit(solution)/shard_map/while
  584.7 45.6 %slice-start = ((s8[5767168]{0:T(1024)(128)(4,1)}), s8[4194304]{0:T(1024)(128)(4,1)S(1)}, s32[]{:S(2)}) async-start(s8[5767168]{0:T(1024)(128)(4,1)} %bitcast.208), calls=%async_computation.3 | async-start | bytes 8388608 | tf_op jit(solution)/shard_map/while
  606.2 21.6 %slice-start.3 = ((s8[5767168]{0:T(1024)(128)(4,1)}), s8[1572864]{0:T(1024)(128)(4,1)S(1)}, s32[]{:S(2)}) async-start(s8[5767168]{0:T(1024)(128)(4,1)} %bitcast.210), calls=%async_computation.6 | async-start | bytes 3145728 | tf_op jit(solution)/shard_map/while
  606.2 24.2 %slice-start.1 = ((s8[5767168]{0:T(1024)(128)(4,1)}), s8[1572864]{0:T(1024)(128)(4,1)S(1)}, s32[]{:S(2)}) async-start(s8[5767168]{0:T(1024)(128)(4,1)} %bitcast.208), calls=%async_computation.4 | async-start | bytes 3145728 | tf_op jit(solution)/shard_map/while
  632.8 21.2 %copy-start = (f32[11,32,32,128]{3,2,1,0:T(8,128)}, f32[11,32,32,128]{3,2,1,0:T(8,128)S(1)}, u32[]{:S(2)}) copy-start(f32[11,32,32,128]{3,2,1,0:T(8,128)S(1)} %convolution_subtract_fusion.4) | copy-start | bytes 17301508 | tf_op jit(solution)/shard_map/while
  693.3 5.7 copy-start.1
  697.0 5.9 copy-start.2
  702.9 1.3 copy-start.4
  707.8 6.8 copy-start.3
  749.3 43.0 %slice-start.2 = ((s8[5767168]{0:T(1024)(128)(4,1)}), s8[4194304]{0:T(1024)(128)(4,1)S(1)}, s32[]{:S(2)}) async-start(s8[5767168]{0:T(1024)(128)(4,1)} %bitcast.210), calls=%async_computation.5 | async-start | bytes 8388608 | tf_op jit(solution)/shard_map/while
  749.3 45.6 %slice-start = ((s8[5767168]{0:T(1024)(128)(4,1)}), s8[4194304]{0:T(1024)(128)(4,1)S(1)}, s32[]{:S(2)}) async-start(s8[5767168]{0:T(1024)(128)(4,1)} %bitcast.208), calls=%async_computation.3 | async-start | bytes 8388608 | tf_op jit(solution)/shard_map/while
  771.0 21.3 %slice-start.3 = ((s8[5767168]{0:T(1024)(128)(4,1)}), s8[1572864]{0:T(1024)(128)(4,1)S(1)}, s32[]{:S(2)}) async-start(s8[5767168]{0:T(1024)(128)(4,1)} %bitcast.210), calls=%async_computation.6 | async-start | bytes 3145728 | tf_op jit(solution)/shard_map/while
  771.0 23.9 %slice-start.1 = ((s8[5767168]{0:T(1024)(128)(4,1)}), s8[1572864]{0:T(1024)(128)(4,1)S(1)}, s32[]{:S(2)}) async-start(s8[5767168]{0:T(1024)(128)(4,1)} %bitcast.208), calls=%async_computation.4 | async-start | bytes 3145728 | tf_op jit(solution)/shard_map/while
  797.4 21.2 %copy-start = (f32[11,32,32,128]{3,2,1,0:T(8,128)}, f32[11,32,32,128]{3,2,1,0:T(8,128)S(1)}, u32[]{:S(2)}) copy-start(f32[11,32,32,128]{3,2,1,0:T(8,128)S(1)} %convolution_subtract_fusion.4) | copy-start | bytes 17301508 | tf_op jit(solution)/shard_map/while
  857.9 5.7 copy-start.1
  861.6 5.9 copy-start.2
  867.5 1.3 copy-start.4
  872.6 6.8 copy-start.3
  914.0 43.1 %slice-start.2 = ((s8[5767168]{0:T(1024)(128)(4,1)}), s8[4194304]{0:T(1024)(128)(4,1)S(1)}, s32[]{:S(2)}) async-start(s8[5767168]{0:T(1024)(128)(4,1)} %bitcast.210), calls=%async_computation.5 | async-start | bytes 8388608 | tf_op jit(solution)/shard_map/while
  914.0 45.6 %slice-start = ((s8[5767168]{0:T(1024)(128)(4,1)}), s8[4194304]{0:T(1024)(128)(4,1)S(1)}, s32[]{:S(2)}) async-start(s8[5767168]{0:T(1024)(128)(4,1)} %bitcast.208), calls=%async_computation.3 | async-start | bytes 8388608 | tf_op jit(solution)/shard_map/while
  935.4 21.6 %slice-start.3 = ((s8[5767168]{0:T(1024)(128)(4,1)}), s8[1572864]{0:T(1024)(128)(4,1)S(1)}, s32[]{:S(2)}) async-start(s8[5767168]{0:T(1024)(128)(4,1)} %bitcast.210), calls=%async_computation.6 | async-start | bytes 3145728 | tf_op jit(solution)/shard_map/while
  935.4 24.2 %slice-start.1 = ((s8[5767168]{0:T(1024)(128)(4,1)}), s8[1572864]{0:T(1024)(128)(4,1)S(1)}, s32[]{:S(2)}) async-start(s8[5767168]{0:T(1024)(128)(4,1)} %bitcast.208), calls=%async_computation.4 | async-start | bytes 3145728 | tf_op jit(solution)/shard_map/while
  962.1 21.2 %copy-start = (f32[11,32,32,128]{3,2,1,0:T(8,128)}, f32[11,32,32,128]{3,2,1,0:T(8,128)S(1)}, u32[]{:S(2)}) copy-start(f32[11,32,32,128]{3,2,1,0:T(8,128)S(1)} %convolution_subtract_fusion.4) | copy-start | bytes 17301508 | tf_op jit(solution)/shard_map/while
  1022.6 5.7 copy-start.1
  1026.3 5.9 copy-start.2
  1032.2 1.3 copy-start.4
  1037.1 6.8 copy-start.3
  1209.8 144.4 %all-to-all-start = ((f32[6,32,128,128]{3,1,0,2:T(8,128)}), f32[6,32,128,128]{3,1,0,2:T(8,128)}, u32[]{:S(2)}, u32[]{:S(2)}) async-start(f32[6,32,128,128]{3,1,0,2:T(8,128)} %get-tuple-element.91), calls=%async_computation | async-start | bytes 25165824 | tf_op jit(solution)/shard_map/all_to_all | solution.py:91
Sparse Core Ops, SparseCore 0:
  13.1 37.9 all-gather.1
where the time goes:
time: 1420 us; the launch traced here: 1410 us
  matrix products  921 us (65%)
  local copies, waits for them, and re-layouts  199 us (14%)
  blocking collectives  154 us (11%)
  waiting for transfers between devices  104 us (7%)
  between operations  14.3 us (1%)
    dot_general x98, matrix products, contract(): return jnp.einsum(form, left, right, precision=TRIPLE)  906 us
    all_to_all x1, blocking collectives, shards(): lax.all_to_all(planes_imag, 'fft', split_axis=2, concat_axis=1, tiled=True)  147 us
    all_to_all x1, waiting for transfers between devices, shards(): lax.all_to_all(planes_real, 'fft', split_axis=2, concat_axis=1, tiled=True)  95.3 us
    dynamic_update_slice x18, local copies, waits for them, and re-layouts, shards(): planes_real, planes_imag = lax.map(one_rotation, (slab_real, slab_imag))  57.8 us
    unnamed x3, local copies, waits for them, and re-layouts  29.4 us
  transfers between devices with their start and end apart: 2, of which 2 were waited for; matrix products, arithmetic and copies ran while one was open for 5% of the time, Pallas kernels for 0%

commit v1 on v0

--- a/solution.py
+++ b/solution.py
@@ -88,7 +88,9 @@
         return inverse_plane(prod_real, prod_imag)
 
     planes_real, planes_imag = lax.map(one_rotation, (slab_real, slab_imag))
-    part_real = lax.all_to_all(planes_real, "fft", split_axis=2, concat_axis=1, tiled=True)
+    cells = jnp.split(planes_real, lax.axis_size("fft"), axis=2)
+    incoming = lax.all_to_all(jnp.stack(cells), "fft", 0, 0)
+    part_real = jnp.concatenate(incoming, axis=1)
     part_imag = lax.all_to_all(planes_imag, "fft", split_axis=2, concat_axis=1, tiled=True)
     field = contract("rkxy,kz->rxyz", part_real, cos_full) - contract(
         "rkxy,kz->rxyz", part_imag, sin_full

time: 1420 us -> 1340 us (0.944)
  blocking collectives: 154 us -> 6.23 us
  waiting for transfers between devices: 104 us -> 225 us
  matrix products: 921 us -> 864 us
    all_to_all x1 -> x0, blocking collectives: 147 us -> none  [shards(): lax.all_to_all(planes_imag, 'fft', split_axis=2, concat_axis=1, tiled=True)]
    all_to_all x1 -> x2, waiting for transfers between devices: 95.3 us -> 217 us  [the longest x1 121 us: shards(): lax.all_to_all(planes_imag, 'fft', split_axis=2, concat_axis=1, tiled=True)]
    dot_general x98, matrix products: 906 us -> 850 us  [contract(): return jnp.einsum(form, left, right, precision=TRIPLE)]
    dynamic_update_slice x18 -> x24, local copies, waits for them, and re-layouts: 57.8 us -> 67.4 us  [shards(): planes_real, planes_imag = lax.map(one_rotation, (slab_real, slab_imag))]
  transfers between devices with their start and end apart: 2 -> 3, of which waited for: 2 -> 3; matrix products, arithmetic and copies ran while one was open for 5% -> 7% of each run, Pallas kernels for 0% -> 0%
where the time goes in v1:
time: 1340 us; the launch traced here: 1330 us
  matrix products  864 us (64%)
  waiting for transfers between devices  225 us (17%)
  local copies, waits for them, and re-layouts  194 us (14%)
  between operations  14.3 us (1%)
    dot_general x98, matrix products, contract(): return jnp.einsum(form, left, right, precision=TRIPLE)  850 us
    all_to_all x1, waiting for transfers between devices, shards(): lax.all_to_all(planes_imag, 'fft', split_axis=2, concat_axis=1, tiled=True)  121 us
    all_to_all x1, waiting for transfers between devices, shards(): incoming = lax.all_to_all(jnp.stack(cells), 'fft', 0, 0)  95.5 us
    dynamic_update_slice x24, local copies, waits for them, and re-layouts, shards(): planes_real, planes_imag = lax.map(one_rotation, (slab_real, slab_imag))  67.4 us
    unnamed x3, local copies, waits for them, and re-layouts  29.4 us
  transfers between devices with their start and end apart: 3, of which 3 were waited for; matrix products, arithmetic and copies ran while one was open for 7% of the time, Pallas kernels for 0%

profile of v1, /device:TPU:0, one launch (start us, length us, event | category | flops | bytes accessed | tf_op | source)
XLA Modules:
  0.0 1333.1 jit_solution(7367252410424921784)
XLA Ops:
  13.2 29.4 %copy.33 = bf16[2,11,32,128,128]{3,4,2,1,0:T(8,128)(2,1)} copy(bf16[2,11,32,128,128]{4,3,2,1,0:T(8,128)(2,1)} %param.5) | data formatting | bytes 46137344
  42.5 8.5 all-gather.2.cloned.1.call-done
  51.1 3.8 fusion.162
  56.3 4.7 subtract_bitcast_fusion.1
  61.0 4.7 add_bitcast_fusion.1
  65.7 929.0 %while.14 = (s32[]{:T(128)}, f32[6,32,128,128]{3,2,1,0:T(8,128)}, f32[6,32,128,128]{3,1,0,2:T(8,128)}, bf16[2,11,32,128,128]{3,4,2,1,0:T(8,128)(2,1)}, f32[6,11,...) while((s32[]{:T(128)}, f32[6,32,128,128]{3,2,1,0:T(8,128)}, ...), condition=%wide.region_3.4_spmd.clone.clone, body=%wide.region_0.3_spmd.clone.clone.sunk | while | flops 8833138688 | bytes 365428992 | solution.py:90
  67.9 3.5 reshape.62
  71.4 3.5 reshape.63
  74.8 5.8 fusion.294
  88.2 21.4 %fusion.293 = f32[11,32,128,128]{3,2,1,0:T(8,128)} fusion(f32[11,32,32,128]{3,2,1,0:T(8,128)S(1)} %convolution_add_fusion.4), kind=kOutput, calls=%fused_computation.58.clone.1 | convolution fusion | flops 1107353600 | bytes 28835840 | tf_op jit(solution)/shard_map/while/body/eval_jaxpr/ckxb,xa->ckab/dot_general | solution.py:23
  109.6 21.2 %fusion.292 = f32[11,32,128,128]{3,2,1,0:T(8,128)} fusion(f32[11,32,32,128]{3,2,1,0:T(8,128)S(1)} %convolution_add_fusion.4), kind=kOutput, calls=%fused_computation.48.clone.1 | convolution fusion | flops 1107353600 | bytes 28835840 | tf_op jit(solution)/shard_map/while/body/eval_jaxpr/ckxb,xa->ckab/dot_general | solution.py:23
  130.8 21.6 %fusion.295 = f32[11,32,128,128]{3,2,1,0:T(8,128)} fusion(f32[11,32,32,128]{3,2,1,0:T(8,128)S(1)} %convolution_subtract_fusion.4), kind=kOutput, calls=%fused_computation.50.clone.1 | convolution fusion | flops 1107353600 | bytes 28835840 | tf_op jit(solution)/shard_map/while/body/eval_jaxpr/ckxb,xa->ckab/dot_general | solution.py:23
  152.4 37.2 %fusion.296 = (f32[32,128,128]{1,2,0:T(8,128)}, f32[32,128,128]{1,2,0:T(8,128)S(1)}) fusion(f32[11,32,128,128]{3,2,1,0:T(8,128)} %fusion.292, bf16[2,11,32,128,128]{3,4,2,1,0:T(8,128)(2,1)} %get-tuple-element.255, f32[11,32,128,128]{3,2,1,0:T(8,128)} %fusion.293, f32[11,32,128,128]{3,2,1,0:T(8,128)} %fusion.295, f32[11,32,32,128]{3,2,1,0:T(8,128)} %copy-done), kind=kOutput, calls=%fused_computation.12.clone.1 | convolution fusion | flops 1175511040 | bytes 102236160 | tf_op jit(solution)/shard_map/while/body/eval_jaxpr/ckxb,xa->ckab/dot_general | solution.py:23
  191.7 3.6 convolution_subtract_fusion.5
  222.3 3.5 reshape.62
  225.8 3.5 reshape.63
  229.3 5.8 fusion.294
  242.7 21.4 %fusion.293 = f32[11,32,128,128]{3,2,1,0:T(8,128)} fusion(f32[11,32,32,128]{3,2,1,0:T(8,128)S(1)} %convolution_add_fusion.4), kind=kOutput, calls=%fused_computation.58.clone.1 | convolution fusion | flops 1107353600 | bytes 28835840 | tf_op jit(solution)/shard_map/while/body/eval_jaxpr/ckxb,xa->ckab/dot_general | solution.py:23
  264.0 21.2 %fusion.292 = f32[11,32,128,128]{3,2,1,0:T(8,128)} fusion(f32[11,32,32,128]{3,2,1,0:T(8,128)S(1)} %convolution_add_fusion.4), kind=kOutput, calls=%fused_computation.48.clone.1 | convolution fusion | flops 1107353600 | bytes 28835840 | tf_op jit(solution)/shard_map/while/body/eval_jaxpr/ckxb,xa->ckab/dot_general | solution.py:23
  285.2 21.4 %fusion.295 = f32[11,32,128,128]{3,2,1,0:T(8,128)} fusion(f32[11,32,32,128]{3,2,1,0:T(8,128)S(1)} %convolution_subtract_fusion.4), kind=kOutput, calls=%fused_computation.50.clone.1 | convolution fusion | flops 1107353600 | bytes 28835840 | tf_op jit(solution)/shard_map/while/body/eval_jaxpr/ckxb,xa->ckab/dot_general | solution.py:23
  306.7 37.5 %fusion.296 = (f32[32,128,128]{1,2,0:T(8,128)}, f32[32,128,128]{1,2,0:T(8,128)S(1)}) fusion(f32[11,32,128,128]{3,2,1,0:T(8,128)} %fusion.292, bf16[2,11,32,128,128]{3,4,2,1,0:T(8,128)(2,1)} %get-tuple-element.255, f32[11,32,128,128]{3,2,1,0:T(8,128)} %fusion.293, f32[11,32,128,128]{3,2,1,0:T(8,128)} %fusion.295, f32[11,32,32,128]{3,2,1,0:T(8,128)} %copy-done), kind=kOutput, calls=%fused_computation.12.clone.1 | convolution fusion | flops 1175511040 | bytes 102236160 | tf_op jit(solution)/shard_map/while/body/eval_jaxpr/ckxb,xa->ckab/dot_general | solution.py:23
  346.1 3.6 convolution_subtract_fusion.5
  376.5 3.5 reshape.62
  380.0 3.5 reshape.63
  383.5 5.8 fusion.294
  396.9 21.6 %fusion.293 = f32[11,32,128,128]{3,2,1,0:T(8,128)} fusion(f32[11,32,32,128]{3,2,1,0:T(8,128)S(1)} %convolution_add_fusion.4), kind=kOutput, calls=%fused_computation.58.clone.1 | convolution fusion | flops 1107353600 | bytes 28835840 | tf_op jit(solution)/shard_map/while/body/eval_jaxpr/ckxb,xa->ckab/dot_general | solution.py:23
  418.5 21.2 %fusion.292 = f32[11,32,128,128]{3,2,1,0:T(8,128)} fusion(f32[11,32,32,128]{3,2,1,0:T(8,128)S(1)} %convolution_add_fusion.4), kind=kOutput, calls=%fused_computation.48.clone.1 | convolution fusion | flops 1107353600 | bytes 28835840 | tf_op jit(solution)/shard_map/while/body/eval_jaxpr/ckxb,xa->ckab/dot_general | solution.py:23
  439.7 21.4 %fusion.295 = f32[11,32,128,128]{3,2,1,0:T(8,128)} fusion(f32[11,32,32,128]{3,2,1,0:T(8,128)S(1)} %convolution_subtract_fusion.4), kind=kOutput, calls=%fused_computation.50.clone.1 | convolution fusion | flops 1107353600 | bytes 28835840 | tf_op jit(solution)/shard_map/while/body/eval_jaxpr/ckxb,xa->ckab/dot_general | solution.py:23
  461.1 37.3 %fusion.296 = (f32[32,128,128]{1,2,0:T(8,128)}, f32[32,128,128]{1,2,0:T(8,128)S(1)}) fusion(f32[11,32,128,128]{3,2,1,0:T(8,128)} %fusion.292, bf16[2,11,32,128,128]{3,4,2,1,0:T(8,128)(2,1)} %get-tuple-element.255, f32[11,32,128,128]{3,2,1,0:T(8,128)} %fusion.293, f32[11,32,128,128]{3,2,1,0:T(8,128)} %fusion.295, f32[11,32,32,128]{3,2,1,0:T(8,128)} %copy-done), kind=kOutput, calls=%fused_computation.12.clone.1 | convolution fusion | flops 1175511040 | bytes 102236160 | tf_op jit(solution)/shard_map/while/body/eval_jaxpr/ckxb,xa->ckab/dot_general | solution.py:23
  500.3 3.6 convolution_subtract_fusion.5
  530.9 3.5 reshape.62
  534.4 3.5 reshape.63
  537.9 5.8 fusion.294
  551.3 21.4 %fusion.293 = f32[11,32,128,128]{3,2,1,0:T(8,128)} fusion(f32[11,32,32,128]{3,2,1,0:T(8,128)S(1)} %convolution_add_fusion.4), kind=kOutput, calls=%fused_computation.58.clone.1 | convolution fusion | flops 1107353600 | bytes 28835840 | tf_op jit(solution)/shard_map/while/body/eval_jaxpr/ckxb,xa->ckab/dot_general | solution.py:23
  572.7 21.2 %fusion.292 = f32[11,32,128,128]{3,2,1,0:T(8,128)} fusion(f32[11,32,32,128]{3,2,1,0:T(8,128)S(1)} %convolution_add_fusion.4), kind=kOutput, calls=%fused_computation.48.clone.1 | convolution fusion | flops 1107353600 | bytes 28835840 | tf_op jit(solution)/shard_map/while/body/eval_jaxpr/ckxb,xa->ckab/dot_general | solution.py:23
  593.9 21.6 %fusion.295 = f32[11,32,128,128]{3,2,1,0:T(8,128)} fusion(f32[11,32,32,128]{3,2,1,0:T(8,128)S(1)} %convolution_subtract_fusion.4), kind=kOutput, calls=%fused_computation.50.clone.1 | convolution fusion | flops 1107353600 | bytes 28835840 | tf_op jit(solution)/shard_map/while/body/eval_jaxpr/ckxb,xa->ckab/dot_general | solution.py:23
  615.5 37.2 %fusion.296 = (f32[32,128,128]{1,2,0:T(8,128)}, f32[32,128,128]{1,2,0:T(8,128)S(1)}) fusion(f32[11,32,128,128]{3,2,1,0:T(8,128)} %fusion.292, bf16[2,11,32,128,128]{3,4,2,1,0:T(8,128)(2,1)} %get-tuple-element.255, f32[11,32,128,128]{3,2,1,0:T(8,128)} %fusion.293, f32[11,32,128,128]{3,2,1,0:T(8,128)} %fusion.295, f32[11,32,32,128]{3,2,1,0:T(8,128)} %copy-done), kind=kOutput, calls=%fused_computation.12.clone.1 | convolution fusion | flops 1175511040 | bytes 102236160 | tf_op jit(solution)/shard_map/while/body/eval_jaxpr/ckxb,xa->ckab/dot_general | solution.py:23
  654.7 3.6 convolution_subtract_fusion.5
  685.4 3.5 reshape.62
  692.4 5.8 fusion.294
  705.8 21.4 %fusion.293 = f32[11,32,128,128]{3,2,1,0:T(8,128)} fusion(f32[11,32,32,128]{3,2,1,0:T(8,128)S(1)} %convolution_add_fusion.4), kind=kOutput, calls=%fused_computation.58.clone.1 | convolution fusion | flops 1107353600 | bytes 28835840 | tf_op jit(solution)/shard_map/while/body/eval_jaxpr/ckxb,xa->ckab/dot_general | solution.py:23
  727.2 21.2 %fusion.292 = f32[11,32,128,128]{3,2,1,0:T(8,128)} fusion(f32[11,32,32,128]{3,2,1,0:T(8,128)S(1)} %convolution_add_fusion.4), kind=kOutput, calls=%fused_computation.48.clone.1 | convolution fusion | flops 1107353600 | bytes 28835840 | tf_op jit(solution)/shard_map/while/body/eval_jaxpr/ckxb,xa->ckab/dot_general | solution.py:23
  748.4 21.4 %fusion.295 = f32[11,32,128,128]{3,2,1,0:T(8,128)} fusion(f32[11,32,32,128]{3,2,1,0:T(8,128)S(1)} %convolution_subtract_fusion.4), kind=kOutput, calls=%fused_computation.50.clone.1 | convolution fusion | flops 1107353600 | bytes 28835840 | tf_op jit(solution)/shard_map/while/body/eval_jaxpr/ckxb,xa->ckab/dot_general | solution.py:23
  769.8 37.5 %fusion.296 = (f32[32,128,128]{1,2,0:T(8,128)}, f32[32,128,128]{1,2,0:T(8,128)S(1)}) fusion(f32[11,32,128,128]{3,2,1,0:T(8,128)} %fusion.292, bf16[2,11,32,128,128]{3,4,2,1,0:T(8,128)(2,1)} %get-tuple-element.255, f32[11,32,128,128]{3,2,1,0:T(8,128)} %fusion.293, f32[11,32,128,128]{3,2,1,0:T(8,128)} %fusion.295, f32[11,32,32,128]{3,2,1,0:T(8,128)} %copy-done), kind=kOutput, calls=%fused_computation.12.clone.1 | convolution fusion | flops 1175511040 | bytes 102236160 | tf_op jit(solution)/shard_map/while/body/eval_jaxpr/ckxb,xa->ckab/dot_general | solution.py:23
  809.2 3.6 convolution_subtract_fusion.5
  839.7 3.5 reshape.62
  843.2 3.5 reshape.63
  846.6 5.8 fusion.294
  860.1 21.6 %fusion.293 = f32[11,32,128,128]{3,2,1,0:T(8,128)} fusion(f32[11,32,32,128]{3,2,1,0:T(8,128)S(1)} %convolution_add_fusion.4), kind=kOutput, calls=%fused_computation.58.clone.1 | convolution fusion | flops 1107353600 | bytes 28835840 | tf_op jit(solution)/shard_map/while/body/eval_jaxpr/ckxb,xa->ckab/dot_general | solution.py:23
  881.7 21.2 %fusion.292 = f32[11,32,128,128]{3,2,1,0:T(8,128)} fusion(f32[11,32,32,128]{3,2,1,0:T(8,128)S(1)} %convolution_add_fusion.4), kind=kOutput, calls=%fused_computation.48.clone.1 | convolution fusion | flops 1107353600 | bytes 28835840 | tf_op jit(solution)/shard_map/while/body/eval_jaxpr/ckxb,xa->ckab/dot_general | solution.py:23
  902.9 21.4 %fusion.295 = f32[11,32,128,128]{3,2,1,0:T(8,128)} fusion(f32[11,32,32,128]{3,2,1,0:T(8,128)S(1)} %convolution_subtract_fusion.4), kind=kOutput, calls=%fused_computation.50.clone.1 | convolution fusion | flops 1107353600 | bytes 28835840 | tf_op jit(solution)/shard_map/while/body/eval_jaxpr/ckxb,xa->ckab/dot_general | solution.py:23
  924.2 37.3 %fusion.296 = (f32[32,128,128]{1,2,0:T(8,128)}, f32[32,128,128]{1,2,0:T(8,128)S(1)}) fusion(f32[11,32,128,128]{3,2,1,0:T(8,128)} %fusion.292, bf16[2,11,32,128,128]{3,4,2,1,0:T(8,128)(2,1)} %get-tuple-element.255, f32[11,32,128,128]{3,2,1,0:T(8,128)} %fusion.293, f32[11,32,128,128]{3,2,1,0:T(8,128)} %fusion.295, f32[11,32,32,128]{3,2,1,0:T(8,128)} %copy-done), kind=kOutput, calls=%fused_computation.12.clone.1 | convolution fusion | flops 1175511040 | bytes 102236160 | tf_op jit(solution)/shard_map/while/body/eval_jaxpr/ckxb,xa->ckab/dot_general | solution.py:23
  963.5 3.6 convolution_subtract_fusion.5
  994.7 6.3 all-to-all-start.1
  1001.0 9.0 slice_bitcast_fusion.3
  1010.0 7.7 pad_maximum_fusion
  1017.7 121.4 %all-to-all-done.1 = f32[6,32,128,128]{3,1,0,2:T(8,128)} async-done(((f32[6,32,128,128]{3,1,0,2:T(8,128)}), f32[6,32,128,128]{3,1,0,2:T(8,128)}, u32[]{:S(2)}, u32[]{:S(2)}) %all-to-all-start.1) | async-done | bytes 12582944 | tf_op jit(solution)/shard_map/all_to_all | solution.py:94
  1139.1 6.8 all-to-all-start
  1145.9 20.2 %copy.42 = f32[6,4,32,32,128]{4,3,2,1,0:T(8,128)} copy(f32[6,4,32,32,128]{4,2,0,3,1:T(8,128)} %bitcast.20) | data formatting | bytes 25165824 | tf_op jit(solution)/shard_map/all_to_all | solution.py:94
  1166.1 22.5 %fusion.134 = f32[6,32,128,128]{3,2,1,0:T(8,128)} fusion(f32[6,128,32,128]{3,2,1,0:T(8,128)} %bitcast.220), kind=kOutput, calls=%fused_computation.136 | convolution fusion | flops 2416148480 | bytes 25165824 | tf_op jit(solution)/shard_map/rkxy,kz->rxyz/dot_general | solution.py:23
  1188.5 95.5 %all-to-all-done = f32[4,6,32,32,128]{4,3,2,1,0:T(8,128)} async-done(((f32[4,6,32,32,128]{4,3,2,1,0:T(8,128)}), f32[4,6,32,32,128]{4,3,2,1,0:T(8,128)}, u32[]{:S(2)}, u32[]{:S(2)}) %all-to-all-start) | async-done | bytes 12582944 | tf_op jit(solution)/shard_map/all_to_all | solution.py:92
  1284.0 11.3 copy.38
  1295.3 24.5 %fusion.198 = (f32[6]{0:T(128)S(1)}, f32[6,32,128,128]{3,2,1,0:T(8,128)}) fusion(f32[6,32,128,128]{3,2,1,0:T(8,128)} %fusion.134, f32[6,128,32,128]{3,2,1,0:T(8,128)} %bitcast.219), kind=kOutput, calls=%fused_computation.210 | convolution fusion | flops 2425585664 | bytes 37748760 | tf_op jit(solution)/shard_map/rkxy,kz->rxyz/dot_general | solution.py:23
  1319.8 6.2 pmin.7
  (189 shorter events, 227.7 us)
Async XLA Ops:
  7.2 43.9 %all-gather.2.cloned.1.call-start = ((), (), s32[]{:S(2)}) async-start(), calls=%async_computation.2 | async-start | bytes 5406720 | tf_op jit(solution)/shard_map/all_gather | solution.py:46
  51.1 3.8 copy-start.2
  71.4 9.3 slice-start
  74.8 5.9 slice-start.1
  74.8 10.9 slice-start.2
  80.7 5.0 slice-start.3
  83.2 47.6 %copy-start = (f32[11,32,32,128]{3,2,1,0:T(8,128)}, f32[11,32,32,128]{3,2,1,0:T(8,128)S(1)}, u32[]{:S(2)}) copy-start(f32[11,32,32,128]{3,2,1,0:T(8,128)S(1)} %convolution_subtract_fusion.4) | copy-start | bytes 17301508 | tf_op jit(solution)/shard_map/while
  189.7 5.6 copy-start.1
  225.8 9.3 slice-start
  229.2 5.9 slice-start.1
  229.2 10.9 slice-start.2
  235.1 5.0 slice-start.3
  237.6 47.6 %copy-start = (f32[11,32,32,128]{3,2,1,0:T(8,128)}, f32[11,32,32,128]{3,2,1,0:T(8,128)S(1)}, u32[]{:S(2)}) copy-start(f32[11,32,32,128]{3,2,1,0:T(8,128)S(1)} %convolution_subtract_fusion.4) | copy-start | bytes 17301508 | tf_op jit(solution)/shard_map/while
  344.1 5.6 copy-start.1
  380.0 9.3 slice-start
  383.5 5.9 slice-start.1
  383.5 10.9 slice-start.2
  389.3 5.0 slice-start.3
  391.8 47.8 %copy-start = (f32[11,32,32,128]{3,2,1,0:T(8,128)}, f32[11,32,32,128]{3,2,1,0:T(8,128)S(1)}, u32[]{:S(2)}) copy-start(f32[11,32,32,128]{3,2,1,0:T(8,128)S(1)} %convolution_subtract_fusion.4) | copy-start | bytes 17301508 | tf_op jit(solution)/shard_map/while
  498.3 5.6 copy-start.1
  534.4 9.3 slice-start
  537.9 5.9 slice-start.1
  537.9 10.9 slice-start.2
  543.8 5.0 slice-start.3
  546.3 47.6 %copy-start = (f32[11,32,32,128]{3,2,1,0:T(8,128)}, f32[11,32,32,128]{3,2,1,0:T(8,128)S(1)}, u32[]{:S(2)}) copy-start(f32[11,32,32,128]{3,2,1,0:T(8,128)S(1)} %convolution_subtract_fusion.4) | copy-start | bytes 17301508 | tf_op jit(solution)/shard_map/while
  652.7 5.6 copy-start.1
  688.9 9.3 slice-start
  692.4 5.9 slice-start.1
  692.4 10.9 slice-start.2
  698.3 5.0 slice-start.3
  700.8 47.6 %copy-start = (f32[11,32,32,128]{3,2,1,0:T(8,128)}, f32[11,32,32,128]{3,2,1,0:T(8,128)S(1)}, u32[]{:S(2)}) copy-start(f32[11,32,32,128]{3,2,1,0:T(8,128)S(1)} %convolution_subtract_fusion.4) | copy-start | bytes 17301508 | tf_op jit(solution)/shard_map/while
  807.2 5.6 copy-start.1
  843.2 9.3 slice-start
  846.6 5.9 slice-start.1
  846.6 10.9 slice-start.2
  852.5 5.0 slice-start.3
  855.0 47.8 %copy-start = (f32[11,32,32,128]{3,2,1,0:T(8,128)}, f32[11,32,32,128]{3,2,1,0:T(8,128)S(1)}, u32[]{:S(2)}) copy-start(f32[11,32,32,128]{3,2,1,0:T(8,128)S(1)} %convolution_subtract_fusion.4) | copy-start | bytes 17301508 | tf_op jit(solution)/shard_map/while
  961.5 5.6 copy-start.1
  994.7 144.4 %all-to-all-start.1 = ((f32[6,32,128,128]{3,1,0,2:T(8,128)}), f32[6,32,128,128]{3,1,0,2:T(8,128)}, u32[]{:S(2)}, u32[]{:S(2)}) async-start(f32[6,32,128,128]{3,1,0,2:T(8,128)} %get-tuple-element.92), calls=%async_computation.1 | async-start | bytes 25165824 | tf_op jit(solution)/shard_map/all_to_all | solution.py:94
  1139.1 144.9 %all-to-all-start = ((f32[4,6,32,32,128]{4,3,2,1,0:T(8,128)}), f32[4,6,32,32,128]{4,3,2,1,0:T(8,128)}, u32[]{:S(2)}, u32[]{:S(2)}) async-start(f32[4,6,32,32,128]{4,3,2,1,0:T(8,128)} %pad_maximum_fusion), calls=%async_computation | async-start | bytes 25165824 | tf_op jit(solution)/shard_map/all_to_all | solution.py:92
Sparse Core Ops, SparseCore 0:
  13.1 37.9 all-gather.1
